TPU v7x, 512 devices: a whole 4x8x8 slice. The times are simulated.
512 devices in a mesh: row: 32 (over y_hi, z, core), col: 16 (over x, y_lo).
Axes of the slice: x: 4, y: 8 (y_hi: 2, y_lo: 4; y = y_hi * 4 + y_lo), z: 8, core: 2. Of those that a mesh axis runs over, the one named last changes fastest.
Arguments:
- inputs: bfloat16 [2048, 12288], P('col', 'row'), may hold values from -0.29882812 to 0.29882812
- preact: bfloat16 [2048, 24576], P('row', 'col'), may hold values from -8 to 8
- out_grad: bfloat16 [2048, 24576], P('row', 'col'), may hold values from -6 to 6
- weight: bfloat16 [12288, 24576], P('row', 'col'), may hold values from -0.0546875 to 0.0546875
Outputs:
- input_grad: bfloat16 [2048, 12288], P('col', 'row')
- weight_grad: float32 [12288, 24576], P('row', 'col')
All inputs are finite; a program needn't handle non-finite values.
Results may differ from a plain program's by a relative error of at most 0.0049.
Values may be sent and summed in bfloat16 or wider, within the bound.
A program may use at most 64 MiB of HBM per device.

v0:
```python
import math

import jax
import jax.numpy as jnp
from jax import lax
from jax.sharding import PartitionSpec as P


def gelu_slope(preact_f):
    coeff = math.sqrt(2.0 / math.pi)
    inner = coeff * (preact_f + 0.044715 * preact_f * preact_f * preact_f)
    tanh_val = jnp.tanh(inner)
    return 0.5 * (1.0 + tanh_val) + 0.5 * preact_f * (1.0 - tanh_val * tanh_val) * coeff * (
        1.0 + 3.0 * 0.044715 * preact_f * preact_f
    )


def hidden_of(grad_part, preact_part):
    return (grad_part.astype(jnp.float32) * gelu_slope(preact_part.astype(jnp.float32))).astype(
        jnp.bfloat16
    )


def shards(inputs, preact, out_grad, weight):
    tokens_all = lax.all_gather(inputs, "col", axis=0, tiled=True)
    local_grad = hidden_of(out_grad, preact)
    grad_all = lax.all_gather(local_grad, "row", axis=0, tiled=True)
    weight_grad = lax.dot_general(
        tokens_all, grad_all, (((0,), (0,)), ((), ())), preferred_element_type=jnp.float32
    )
    input_grad = lax.psum_scatter(
        lax.dot_general(
            grad_all, weight, (((1,), (1,)), ((), ())), preferred_element_type=jnp.float32
        ),
        "col",
        scatter_dimension=0,
        tiled=True,
    ).astype(jnp.bfloat16)
    return (input_grad, weight_grad)


def solution(mesh):
    in_specs = (P("col", "row"), P("row", "col"), P("row", "col"), P("row", "col"))
    out_specs = (P("col", "row"), P("row", "col"))
    return jax.shard_map(shards, mesh=mesh, in_specs=in_specs, out_specs=out_specs, check_vma=False)
```

profile of v0, /device:TPU:6, one launch (start us, length us, event | category | flops | bytes accessed | tf_op | source)
XLA Modules:
  0.0 322.6 jit_solution(13602441151451360976)
XLA Ops:
  7.2 0.0 copy-start
  7.2 0.0 all-gather.3.cloned.1.call-start
  7.2 2.1 fusion.7
  9.3 0.0 all-gather.3.cloned.1.call-update
  9.3 0.0 all-gather.5.cloned.1.call-start
  9.4 0.7 all-gather.5.cloned.1.call-update
  10.1 0.0 reduce-scatter.2.cloned.1.call-start
  10.1 123.5 %all-gather.3.cloned.1.call-done = bf16[2048,1536]{1,0:T(8,128)(2,1)} async-done(((bf16[64,1536]{1,0:T(8,128)(2,1)}), bf16[2048,1536]{1,0:T(8,128)(2,1)}) %all-gather.3.cloned.1.call-update) | async-done | bytes 6291472 | tf_op jit(solution)/shard_map/all_gather | solution.py:27
  133.6 0.0 copy-done
  133.6 7.9 %fusion.9 = f32[2048,384]{1,0:T(8,128)} fusion(bf16[2048,1536]{1,0:T(8,128)(2,1)} %all-gather.3.cloned.1.call-done, bf16[384,1536]{1,0:T(8,128)(2,1)S(1)} %copy-done), kind=kOutput, calls=%fused_computation.17 | convolution fusion | flops 2415919104 | bytes 10616832 | tf_op jit(solution)/shard_map/dot_general | solution.py:32
  141.5 0.0 reduce-scatter.2.cloned.1.call-update
  141.5 73.2 %all-gather.5.cloned.1.call-done = bf16[2048,384]{1,0:T(8,128)(2,1)} async-done(((bf16[128,384]{1,0:T(8,128)(2,1)}), bf16[2048,384]{1,0:T(8,128)(2,1)}) %all-gather.5.cloned.1.call-update) | async-done | bytes 1572880 | tf_op jit(solution)/shard_map/all_gather | solution.py:25
  214.8 6.0 %convolution_bitcast_fusion = f32[384,1536]{0,1:T(8,128)S(1)} fusion(bf16[2048,1536]{1,0:T(8,128)(2,1)} %all-gather.3.cloned.1.call-done, bf16[2048,384]{1,0:T(8,128)(2,1)} %all-gather.5.cloned.1.call-done), kind=kOutput, calls=%fused_computation | convolution fusion | flops 2415919104 | bytes 10223616 | tf_op jit(solution)/shard_map/dot_general | solution.py:28
  220.8 2.0 copy.6
  222.7 91.8 %reduce-scatter.2.cloned.1.call-done = f32[128,384]{1,0:T(8,128)} async-done(((f32[2048,384]{1,0:T(8,128)}), f32[128,384]{1,0:T(8,128)}) %reduce-scatter.2.cloned.1.call-update) | async-done | bytes 196624 | tf_op jit(solution)/shard_map/reduce_scatter | solution.py:31
  314.5 1.6 convert_element_type.15
Async XLA Ops:
  7.2 126.4 %copy-start = (bf16[384,1536]{1,0:T(8,128)(2,1)S(1)}, bf16[384,1536]{1,0:T(8,128)(2,1)}, u32[]{:S(2)}) copy-start(bf16[384,1536]{1,0:T(8,128)(2,1)} %param.7) | copy-start | bytes 3538948
  7.2 126.4 %all-gather.3.cloned.1.call-start = ((), (), s32[]{:S(2)}) async-start(), calls=%async_computation.1 | async-start | bytes 6488064 | tf_op jit(solution)/shard_map/all_gather | solution.py:27
  9.3 205.4 %all-gather.5.cloned.1.call-start = ((), (), s32[]{:S(2)}) async-start(), calls=%async_computation.3 | async-start | bytes 1671168 | tf_op jit(solution)/shard_map/all_gather | solution.py:25
  10.1 304.4 %reduce-scatter.2.cloned.1.call-start = ((), (), s32[]{:S(2)}) async-start(), calls=%async_computation.2 | async-start | bytes 3342336 | tf_op jit(solution)/shard_map/reduce_scatter | solution.py:31
Sparse Core Ops, SparseCore 0:
  11.9 121.5 all-gather.2
  135.7 79.0 all-gather.4
  217.6 96.8 reduce-scatter.1
where the time goes:
time: 329 us; the launch traced here: 323 us
  waiting for transfers between devices  289 us (88%)
  matrix products  13.9 us (4%)
  between operations  13.8 us (4%)
  other arithmetic  3.64 us (1%)
    all_gather x1, waiting for transfers between devices, shards(): grad_all = lax.all_gather(local_grad, 'row', axis=0, tiled=True)  123 us
    reduce_scatter x1, waiting for transfers between devices, shards(): lax.psum_scatter(lax.dot_general(grad_all, weight, (((1,), (1,)), ((), ()...  91.8 us
    all_gather x1, waiting for transfers between devices, shards(): tokens_all = lax.all_gather(inputs, 'col', axis=0, tiled=True)  73.2 us
    dot_general x1, matrix products, shards(): lax.dot_general(grad_all, weight, (((1,), (1,)), ((), ())), preferred_ele...  7.93 us
  transfers between devices with their start and end apart: 3, of which 3 were waited for; matrix products, arithmetic and copies ran while one was open for 5% of the time, Pallas kernels for 0%

commit v1 on v0

v1 whole, which is shorter than its diff:
```python
import functools
import math

import jax
import jax.numpy as jnp
from jax import lax
from jax.experimental import pallas as pl
from jax.experimental.pallas import tpu as pltpu
from jax.sharding import PartitionSpec as P

MESH = pl.DeviceIdType.MESH
F32, BF16 = jnp.float32, jnp.bfloat16

NX, NYL, NYH, NZ = 4, 4, 2, 8
ROWS, HID, WID = 64, 1536, 384
CHUNK = ROWS // 2
TOK = 2 * ROWS
TOKENS = TOK * NYH * NZ
RIGHT, LEFT = 0, 1


def gelu_slope(preact_f):
    coeff = math.sqrt(2.0 / math.pi)
    inner = coeff * (preact_f + 0.044715 * preact_f * preact_f * preact_f)
    tanh_val = jnp.tanh(inner)
    return 0.5 * (1.0 + tanh_val) + 0.5 * preact_f * (1.0 - tanh_val * tanh_val) * coeff * (
        1.0 + 3.0 * 0.044715 * preact_f * preact_f
    )


def kernel(
    x_ref, pre_ref, grad_ref, w_hbm, ig_ref, wg_hbm,
    h, xs, w, xt, wg, g_own, g_out, g_in, s_out, s_in, g_fin,
    w_sem, wg_sem,
    hy_send, hy_recv, hz_send, hz_recv, hc_send, hc_recv,
    xy_send, xy_recv, xx_send, xx_recv,
    gx_send, gx_recv, gy_send, gy_recv,
):
    r, c = lax.axis_index("row"), lax.axis_index("col")
    yh, z, core = r // (2 * NZ), (r // 2) % NZ, r % 2
    x, yl = c // NYL, c % NYL

    def dev(yh_=yh, z_=z, core_=core, x_=x, yl_=yl):
        return ((yh_ * NZ + z_) * 2 + core_, x_ * NYL + yl_)

    def copy(src, dst, ssem, rsem, to):
        return pltpu.make_async_remote_copy(
            src_ref=src, dst_ref=dst, send_sem=ssem, recv_sem=rsem, device_id=to, device_id_type=MESH
        )

    w_copy = pltpu.make_async_copy(w_hbm, w, w_sem)
    w_copy.start()

    partner = dev(yh_=1 - yh)
    sibling = dev(core_=1 - core)
    ahead, behind = dev(z_=(z + 1) % NZ), dev(z_=(z + NZ - 1) % NZ)
    peers = [partner, sibling, ahead, behind]
    peers += [dev(x_=(x + d) % NX) for d in range(1, NX)]
    peers += [dev(yl_=(yl + d) % NYL) for d in range(1, NYL)]
    barrier = pltpu.get_barrier_semaphore()
    for peer in peers:
        pl.semaphore_signal(barrier, inc=1, device_id=peer, device_id_type=MESH)

    def rows(yh_, z_, core_, chunk=None):
        base = ((yh_ * NZ + z_) * 2 + core_) * ROWS
        if chunk is None:
            return pl.ds(pl.multiple_of(base, ROWS), ROWS)
        return pl.ds(pl.multiple_of(base + chunk * CHUNK, CHUNK), CHUNK)

    def side(s):
        return yh if s == 0 else 1 - yh

    def make_hidden(chunk):
        at = pl.ds(chunk * CHUNK, CHUNK)
        h[rows(yh, z, core, chunk), :] = (
            grad_ref[at, :].astype(F32) * gelu_slope(pre_ref[at, :].astype(F32))
        ).astype(BF16)

    def ring(s, k, way, chunk, z_from):
        block = h.at[rows(side(s), z_from, core, chunk)]
        return copy(
            block, block, hz_send.at[s, way, k, chunk], hz_recv.at[s, way, k, chunk],
            ahead if way == RIGHT else behind,
        )

    def across(chunk, yh_):
        block = h.at[rows(yh_, z, core, chunk)]
        return copy(block, block, hy_send.at[chunk], hy_recv.at[chunk], partner)

    def share(s, slot, z_from, core_):
        block = h.at[rows(side(s), z_from, core_)]
        return copy(block, block, hc_send.at[s, slot], hc_recv.at[s, slot], sibling)

    def origin(way, k):
        return (z + NZ - k) % NZ if way == RIGHT else (z + k) % NZ

    def x_block(x_, yl_):
        return xs.at[pl.ds(pl.multiple_of((x_ * NYL + yl_) * TOK, TOK), TOK)]

    def x_near(d, to_or_from):
        return copy(
            x_ref, x_block(x, to_or_from), xy_send.at[d - 1], xy_recv.at[d - 1], dev(yl_=(yl + d) % NYL)
        )

    def x_far(d, x_):
        block = xs.at[pl.ds(pl.multiple_of(x_ * NYL * TOK, NYL * TOK), NYL * TOK)]
        return copy(block, block, xx_send.at[d - 1], xx_recv.at[d - 1], dev(x_=(x + d) % NX))

    make_hidden(0)
    pl.semaphore_wait(barrier, len(peers))
    for chunk in (0, 1):
        if chunk:
            make_hidden(1)
        across(chunk, yh).start()
        ring(0, 1, RIGHT, chunk, z).start()
        ring(0, 1, LEFT, chunk, z).start()
    share(0, 0, z, core).start()
    for d in range(1, NYL):
        x_near(d, yl).start()
    x_block(x, yl)[...] = x_ref[...]
    w_copy.wait()

    def home(s, z_from):
        return side(s) * (NZ // NYL) + z_from // NYL, z_from % NYL

    def part_out(s, z_from, x_to, j):
        d = (x + NX - x_to) % NX
        at = side(s) * NZ + z_from
        return copy(
            g_out.at[at], g_in.at[d - 1, j], gx_send.at[at], gx_recv.at[d - 1, j], dev(x_=x_to)
        )

    def product(s, slot, z_from):
        share(s, slot, z_from, 1 - core).wait_recv()
        at = pl.ds(pl.multiple_of((side(s) * NZ + z_from) * TOK, TOK), TOK)
        part = lax.dot_general(h[at, :], w[...], (((1,), (1,)), ((), ())), preferred_element_type=F32)
        x_to, j = home(s, z_from)

        @pl.when(x_to == x)
        def _():
            g_own[j] = part

        @pl.when(x_to != x)
        def _():
            g_out[side(s) * NZ + z_from] = part.astype(BF16)
            part_out(s, z_from, x_to, j).start()

    def sum_out(j):
        d = (yl + NYL - j) % NYL
        return copy(s_out.at[j], s_in.at[d - 1], gy_send.at[j], gy_recv.at[d - 1], dev(yl_=j))

    def reduce_x(s, z_from):
        x_to, j = home(s, z_from)

        @pl.when(x_to == x)
        def _():
            total = g_own[j]
            for d in range(1, NX):
                copy(g_out.at[0], g_in.at[d - 1, j], gx_send.at[0], gx_recv.at[d - 1, j], sibling).wait_recv()
                total = total + g_in[d - 1, j].astype(F32)

            @pl.when(j == yl)
            def _():
                g_fin[...] = total

            @pl.when(j != yl)
            def _():
                s_out[j] = total.astype(BF16)
                sum_out(j).start()

    def pass_on(s, k, way, chunk):
        z_from = origin(way, k)
        ring(s, k, way, chunk, z_from).wait_recv()

        @pl.when((k < 3) | (chunk == way))
        def _():
            ring(s, k + 1, way, chunk, z_from).start()

    def forward(s, k):
        for chunk in (0, 1):
            pass_on(s, k, RIGHT, chunk)
            pass_on(s, k, LEFT, chunk)
        share(s, k, origin(RIGHT, k), core).start()
        share(s, 3 + k, origin(LEFT, k), core).start()

    def last(s):
        far = origin(RIGHT, 4)
        ring(s, 4, RIGHT, 0, far).wait_recv()
        ring(s, 4, LEFT, 1, far).wait_recv()
        share(s, 7, far, core).start()

    product(0, 0, z)

    @pl.loop(1, 4)
    def _(k):
        forward(0, k)

        @pl.when(k == 2)
        def _():
            for d in range(1, NYL):
                x_near(d, (yl + NYL - d) % NYL).wait_recv()
            for d in range(1, NX):
                x_far(d, x).start()

        product(0, k, origin(RIGHT, k))
        product(0, 3 + k, origin(LEFT, k))

    for chunk in (0, 1):
        across(chunk, 1 - yh).wait_recv()
        ring(1, 1, RIGHT, chunk, z).start()
        ring(1, 1, LEFT, chunk, z).start()
    share(1, 0, z, core).start()
    last(0)
    product(1, 0, z)
    product(0, 7, origin(RIGHT, 4))
    reduce_x(0, z)

    @pl.loop(1, 4)
    def _(k):
        forward(1, k)
        product(1, k, origin(RIGHT, k))
        product(1, 3 + k, origin(LEFT, k))
        reduce_x(0, origin(RIGHT, k))
        reduce_x(0, origin(LEFT, k))

        @pl.when(k == 1)
        def _():
            reduce_x(0, origin(RIGHT, 4))
            reduce_x(1, z)

        @pl.when(k > 1)
        def _():
            reduce_x(1, origin(RIGHT, k - 1))
            reduce_x(1, origin(LEFT, k - 1))

    last(1)
    product(1, 7, origin(RIGHT, 4))

    for d in range(1, NX):
        x_far(d, (x + NX - d) % NX).wait_recv()
    half = TOKENS // 2
    piece = 384
    n_pieces = HID // piece

    def transpose(yh_):
        at = pl.multiple_of(yh_ * half, half)
        for i in range(half // 256):
            xt[:, pl.ds(i * 256, 256)] = xs[pl.ds(at + i * 256, 256), :].T

    def outer(yh_, n):
        at = pl.ds(pl.multiple_of(yh_ * half, half), half)
        cols = pl.ds(pl.multiple_of(n * piece, piece), piece)
        return cols, jnp.dot(xt[...], h[at, cols], preferred_element_type=F32)

    transpose(yh)

    @pl.loop(0, n_pieces)
    def _(n):
        cols, value = outer(yh, n)
        wg[:, cols] = value

    reduce_x(1, origin(RIGHT, 3))
    reduce_x(1, origin(LEFT, 3))
    reduce_x(1, origin(RIGHT, 4))
    transpose(1 - yh)

    def wg_copy(n):
        cols = pl.ds(pl.multiple_of(n * piece, piece), piece)
        return pltpu.make_async_copy(wg.at[:, cols], wg_hbm.at[:, cols], wg_sem.at[n])

    @pl.loop(0, n_pieces)
    def _(n):
        cols, value = outer(1 - yh, n)
        wg[:, cols] += value
        wg_copy(n).start()

    total = g_fin[...]
    for d in range(1, NYL):
        copy(s_out.at[0], s_in.at[d - 1], gy_send.at[0], gy_recv.at[d - 1], sibling).wait_recv()
        total = total + s_in[d - 1].astype(F32)
    ig_ref[...] = total.astype(BF16)

    for n in range(n_pieces):
        wg_copy(n).wait()
    for chunk in (0, 1):
        across(chunk, yh).wait_send()
    for s in (0, 1):
        for way in (RIGHT, LEFT):
            for k in range(1, 5):
                for chunk in (0, 1):
                    if k < 4 or chunk == way:
                        ring(s, k, way, chunk, z).wait_send()
        for slot in range(8):
            share(s, slot, z, core).wait_send()
    for d in range(1, NYL):
        x_near(d, yl).wait_send()
    for d in range(1, NX):
        x_far(d, x).wait_send()

    @pl.loop(0, NYH * NZ)
    def _(at):
        @pl.when(at // NYL != x)
        def _():
            copy(g_out.at[at], g_in.at[0, 0], gx_send.at[at], gx_recv.at[0, 0], sibling).wait_send()

    @pl.loop(0, NYL)
    def _(j):
        @pl.when(j != yl)
        def _():
            copy(s_out.at[j], s_in.at[0], gy_send.at[j], gy_recv.at[0], sibling).wait_send()


def shards(inputs, preact, out_grad, weight):
    vmem = pl.BlockSpec(memory_space=pltpu.VMEM)
    hbm = pl.BlockSpec(memory_space=pl.ANY)
    dma = pltpu.SemaphoreType.DMA
    return pl.pallas_call(
        kernel,
        out_shape=(jax.ShapeDtypeStruct((TOK, WID), BF16), jax.ShapeDtypeStruct((WID, HID), F32)),
        in_specs=[vmem, vmem, vmem, hbm],
        out_specs=(vmem, hbm),
        scratch_shapes=[
            pltpu.VMEM((TOKENS, HID), BF16),
            pltpu.VMEM((TOKENS, WID), BF16),
            pltpu.VMEM((WID, HID), BF16),
            pltpu.VMEM((WID, TOKENS // 2), BF16),
            pltpu.VMEM((WID, HID), F32),
            pltpu.VMEM((NYL, TOK, WID), F32),
            pltpu.VMEM((NYH * NZ, TOK, WID), BF16),
            pltpu.VMEM((NX - 1, NYL, TOK, WID), BF16),
            pltpu.VMEM((NYL, TOK, WID), BF16),
            pltpu.VMEM((NYL - 1, TOK, WID), BF16),
            pltpu.VMEM((TOK, WID), F32),
            dma(()),
            dma((4,)),
            dma((2,)), dma((2,)),
            dma((2, 2, 5, 2)), dma((2, 2, 5, 2)),
            dma((2, 8)), dma((2, 8)),
            dma((NYL - 1,)), dma((NYL - 1,)),
            dma((NX - 1,)), dma((NX - 1,)),
            dma((NYH * NZ,)), dma((NX - 1, NYL)),
            dma((NYL,)), dma((NYL - 1,)),
        ],
        compiler_params=pltpu.CompilerParams(
            collective_id=0, has_side_effects=True, vmem_limit_bytes=48 << 20
        ),
        cost_estimate=pl.CostEstimate(
            flops=4 * TOKENS * HID * WID, bytes_accessed=8 << 20, transcendentals=ROWS * HID
        ),
    )(inputs, preact, out_grad, weight)


def solution(mesh):
    in_specs = (P("col", "row"), P("row", "col"), P("row", "col"), P("row", "col"))
    out_specs = (P("col", "row"), P("row", "col"))
    return jax.shard_map(shards, mesh=mesh, in_specs=in_specs, out_specs=out_specs, check_vma=False)
```

time: 329 us -> 97.2 us (0.30); the launches traced: 323 us -> 96.8 us
  waiting for transfers between devices: 289 us -> 0 us
  Pallas kernels: 0 us -> 90.1 us
  matrix products: 13.9 us -> 0 us
  between operations: 13.8 us -> 0.65 us
  local copies, waits for them, and re-layouts: 1.96 us -> 6.06 us
  other arithmetic: 3.64 us -> 0 us
    all_gather x2 -> x0, waiting for transfers between devices: 197 us -> none  [the longest x1 123 us: shards(): grad_all = lax.all_gather(local_grad, 'row', axis=0, tiled=True)]
    reduce_scatter x1 -> x0, waiting for transfers between devices: 91.8 us -> none  [shards(): lax.psum_scatter(lax.dot_general(grad_all, weight, (((1,), (1,)), ((), ()...]
    pallas_call x0 -> x1, Pallas kernels: none -> 90.1 us  [shards(): pl.pallas_call(kernel, out_shape=(jax.ShapeDtypeStruct((TOK, WID), BF16),...]
    dot_general x2 -> x0, matrix products: 13.9 us -> none  [the longest x1 7.93 us: shards(): lax.dot_general(grad_all, weight, (((1,), (1,)), ((), ())), preferred_ele...]
    unnamed x3 -> x10, local copies, waits for them, and re-layouts: 1.96 us -> 6.06 us
    convert_element_type x2 -> x0, other arithmetic: 3.64 us -> none  [the longest x1 2.06 us: hidden_of(): (grad_part.astype(jnp.float32) * gelu_slope(preact_part.astype(jnp.float3...]
  transfers between devices with their start and end apart: 3 -> 0, of which waited for: 3 -> 0; matrix products, arithmetic and copies ran while one was open for 5% -> 0% of each run, Pallas kernels for 0% -> 0%
where the time goes in v1:
time: 97.2 us; the launch traced here: 96.8 us
  Pallas kernels  90.1 us (93%)
  local copies, waits for them, and re-layouts  6.06 us (6%)
    pallas_call x1, Pallas kernels, shards(): pl.pallas_call(kernel, out_shape=(jax.ShapeDtypeStruct((TOK, WID), BF16),...  90.1 us
    unnamed x10, local copies, waits for them, and re-layouts  6.06 us

profile of v1, /device:TPU:6, one launch (start us, length us, event | category | flops | bytes accessed | tf_op | source)
XLA Modules:
  0.0 96.8 jit_solution(2777600983657015766)
XLA Ops:
  0.6 0.0 copy-start
  0.6 1.3 %copy-done = bf16[384,1536]{1,0:T(8,128)(2,1)S(1)} copy-done((bf16[384,1536]{1,0:T(8,128)(2,1)S(1)}, bf16[384,1536]{1,0:T(8,128)(2,1)}, u32[]{:S(2)}) %copy-start) | copy-done | bytes 1179672
  1.9 0.0 copy-start.1
  1.9 0.9 copy-done.1
  2.8 0.0 copy-start.2
  2.8 0.9 copy-done.2
  3.8 0.0 copy-start.3
  3.8 0.9 copy-done.3
  4.7 90.1 %shard_map.59 = (bf16[128,384]{1,0:T(8,128)(2,1)S(1)}, f32[384,1536]{1,0:T(8,128)S(1)}) custom-call(bf16[128,384]{1,0:T(8,128)(2,1)S(1)} %copy-done.3, bf16[64,1536]{1,0:T(8,128)(2,1)S(1)} %copy-done.1, bf16[64,1536]{1,0:T(8,128)(2,1)S(1)} %copy-done.2, bf16[384,1536]{1,0:T(8,128)(2,1)S(1)} %copy-done), custom_call_target="tpu_custom_call" | custom-call | flops 4831838208 | bytes 8388608 | tf_op jit(solution)/shard_map/pallas_call | solution.py:317
  94.8 0.6 copy.8
  95.4 1.4 %copy.9 = f32[384,1536]{1,0:T(8,128)} copy(f32[384,1536]{1,0:T(8,128)S(1)} %get-tuple-element.5) | data formatting | bytes 4718592
Async XLA Ops:
  0.6 1.3 %copy-start = (bf16[384,1536]{1,0:T(8,128)(2,1)S(1)}, bf16[384,1536]{1,0:T(8,128)(2,1)}, u32[]{:S(2)}) copy-start(bf16[384,1536]{1,0:T(8,128)(2,1)} %w_hbm.1) | copy-start | bytes 3538948
  1.9 0.9 copy-start.1
  2.8 0.9 copy-start.2
  3.8 0.9 copy-start.3

commit v2 on v1

v2 whole, which is shorter than its diff:
```python
import functools
import math

import jax
import jax.numpy as jnp
from jax import lax
from jax.experimental import pallas as pl
from jax.experimental.pallas import tpu as pltpu
from jax.sharding import PartitionSpec as P

MESH = pl.DeviceIdType.MESH
F32, BF16 = jnp.float32, jnp.bfloat16

NX, NYL, NYH, NZ = 4, 4, 2, 8
ROWS, HID, WID = 64, 1536, 384
NCH = 4
CHUNK = ROWS // NCH
PIECE = 384
TOK = 2 * ROWS
TOKENS = TOK * NYH * NZ
RIGHT, LEFT = 0, 1
PLAN = ('p00', 'f01', 'f02', 'a0', 'a1', 'a2', 'a3', 'c', 'n', 'p01', 'f03', 'p02', 'p10', 'l0', 'f11', 'x1', 'x2', 'x3', 'p03', 'p04', 'f12', 'p11', 'r00', 'r01', 'r02', 'f13', 'p12', 'p13', 'r03', 'r04', 'r10', 'l1', 'p14', 'w', 'r11', 'r12', 't0', 'o004', 'r13', 'r14', 't1', 'o104')
HALF_OF = {RIGHT: range(NCH // 2), LEFT: range(NCH // 2, NCH)}


def gelu_slope(preact_f):
    coeff = math.sqrt(2.0 / math.pi)
    inner = coeff * (preact_f + 0.044715 * preact_f * preact_f * preact_f)
    tanh_val = jnp.tanh(inner)
    return 0.5 * (1.0 + tanh_val) + 0.5 * preact_f * (1.0 - tanh_val * tanh_val) * coeff * (
        1.0 + 3.0 * 0.044715 * preact_f * preact_f
    )


def kernel(
    x_hbm, pre_hbm, grad_hbm, w_hbm, ig_ref, wg,
    pre, grad, h, xs, w, xt, g_own, g_out, g_in, s_out, s_in, g_fin,
    in_sem,
    hy_send, hy_recv, hz_send, hz_recv, hc_send, hc_recv,
    xy_send, xy_recv, xx_send, xx_recv,
    gx_send, gx_recv, gy_send, gy_recv,
):
    r, c = lax.axis_index("row"), lax.axis_index("col")
    yh, z, core = r // (2 * NZ), (r // 2) % NZ, r % 2
    x, yl = c // NYL, c % NYL

    def dev(yh_=yh, z_=z, core_=core, x_=x, yl_=yl):
        return ((yh_ * NZ + z_) * 2 + core_, x_ * NYL + yl_)

    def copy(src, dst, ssem, rsem, to):
        return pltpu.make_async_remote_copy(
            src_ref=src, dst_ref=dst, send_sem=ssem, recv_sem=rsem, device_id=to, device_id_type=MESH
        )

    def x_block(x_, yl_):
        return xs.at[pl.ds(pl.multiple_of((x_ * NYL + yl_) * TOK, TOK), TOK)]

    pre_copy = pltpu.make_async_copy(pre_hbm, pre, in_sem.at[0])
    grad_copy = pltpu.make_async_copy(grad_hbm, grad, in_sem.at[1])
    x_copy = pltpu.make_async_copy(x_hbm, x_block(x, yl), in_sem.at[2])
    w_copy = pltpu.make_async_copy(w_hbm, w, in_sem.at[3])
    for local in (pre_copy, grad_copy, x_copy, w_copy):
        local.start()

    partner = dev(yh_=1 - yh)
    sibling = dev(core_=1 - core)
    ahead, behind = dev(z_=(z + 1) % NZ), dev(z_=(z + NZ - 1) % NZ)
    peers = [partner, sibling, ahead, behind]
    peers += [dev(x_=(x + d) % NX) for d in range(1, NX)]
    peers += [dev(yl_=(yl + d) % NYL) for d in range(1, NYL)]
    barrier = pltpu.get_barrier_semaphore()
    for peer in peers:
        pl.semaphore_signal(barrier, inc=1, device_id=peer, device_id_type=MESH)

    def rows(yh_, z_, core_, chunk=None):
        base = ((yh_ * NZ + z_) * 2 + core_) * ROWS
        if chunk is None:
            return pl.ds(pl.multiple_of(base, ROWS), ROWS)
        return pl.ds(pl.multiple_of(base + chunk * CHUNK, CHUNK), CHUNK)

    def side(s):
        return yh if s == 0 else 1 - yh

    def make_hidden(chunk):
        at = pl.ds(chunk * CHUNK, CHUNK)
        h[rows(yh, z, core, chunk), :] = (
            grad[at, :].astype(F32) * gelu_slope(pre[at, :].astype(F32))
        ).astype(BF16)

    def ring(s, k, way, chunk, z_from):
        block = h.at[rows(side(s), z_from, core, chunk)]
        return copy(
            block, block, hz_send.at[s, way, k, chunk], hz_recv.at[s, way, k, chunk],
            ahead if way == RIGHT else behind,
        )

    def across(chunk, yh_):
        block = h.at[rows(yh_, z, core, chunk)]
        return copy(block, block, hy_send.at[chunk], hy_recv.at[chunk], partner)

    def share(s, slot, z_from, core_):
        block = h.at[rows(side(s), z_from, core_)]
        return copy(block, block, hc_send.at[s, slot], hc_recv.at[s, slot], sibling)

    def origin(way, k):
        return (z + NZ - k) % NZ if way == RIGHT else (z + k) % NZ

    def x_near(d, yl_):
        block = x_block(x, yl_)
        return copy(block, block, xy_send.at[d - 1], xy_recv.at[d - 1], dev(yl_=(yl + d) % NYL))

    def x_far(d, e, x_):
        block = x_block(x_, (yl + NYL - e) % NYL)
        return copy(block, block, xx_send.at[d - 1, e], xx_recv.at[d - 1, e], dev(x_=(x + d) % NX))

    def start_chunk(s, chunk):
        ring(s, 1, RIGHT, chunk, z).start()
        ring(s, 1, LEFT, chunk, z).start()

    pre_copy.wait()
    grad_copy.wait()
    make_hidden(0)
    pl.semaphore_wait(barrier, len(peers))
    for chunk in range(NCH):
        if chunk:
            make_hidden(chunk)
        across(chunk, yh).start()
        start_chunk(0, chunk)
    share(0, 0, z, core).start()
    x_copy.wait()
    for d in range(1, NX):
        x_far(d, 0, x).start()
    w_copy.wait()

    def home(s, z_from):
        return side(s) * (NZ // NYL) + z_from // NYL, z_from % NYL

    def part_out(s, z_from, x_to, j):
        d = (x + NX - x_to) % NX
        at = side(s) * NZ + z_from
        return copy(
            g_out.at[at], g_in.at[d - 1, j], gx_send.at[at], gx_recv.at[d - 1, j], dev(x_=x_to)
        )

    def product(s, slot, z_from):
        share(s, slot, z_from, 1 - core).wait_recv()
        at = pl.ds(pl.multiple_of((side(s) * NZ + z_from) * TOK, TOK), TOK)
        part = lax.dot_general(h[at, :], w[...], (((1,), (1,)), ((), ())), preferred_element_type=F32)
        x_to, j = home(s, z_from)

        @pl.when(x_to == x)
        def _():
            g_own[j] = part

        @pl.when(x_to != x)
        def _():
            g_out[side(s) * NZ + z_from] = part.astype(BF16)
            part_out(s, z_from, x_to, j).start()

    def both(fn):
        @pl.loop(0, 2)
        def _(i):
            fn(i)

    def products(s, k):
        both(lambda i: product(s, k + 3 * i, (z + NZ + (2 * i - 1) * k) % NZ))

    def sum_out(j):
        d = (yl + NYL - j) % NYL
        return copy(s_out.at[j], s_in.at[d - 1], gy_send.at[j], gy_recv.at[d - 1], dev(yl_=j))

    def reduce_x(s, z_from):
        x_to, j = home(s, z_from)

        @pl.when(x_to == x)
        def _():
            total = g_own[j]
            for d in range(1, NX):
                copy(g_out.at[0], g_in.at[d - 1, j], gx_send.at[0], gx_recv.at[d - 1, j], sibling).wait_recv()
                total = total + g_in[d - 1, j].astype(F32)

            @pl.when(j == yl)
            def _():
                g_fin[...] = total

            @pl.when(j != yl)
            def _():
                s_out[j] = total.astype(BF16)
                sum_out(j).start()

    def reduce_pair(s, k):
        both(lambda i: reduce_x(s, (z + NZ + (2 * i - 1) * k) % NZ))

    def forward(s, k):
        for chunk in range(NCH):
            for way in (RIGHT, LEFT):
                z_from = origin(way, k)
                ring(s, k, way, chunk, z_from).wait_recv()
                if k < 3 or chunk in HALF_OF[way]:
                    ring(s, k + 1, way, chunk, z_from).start()
        share(s, k, origin(RIGHT, k), core).start()
        share(s, 3 + k, origin(LEFT, k), core).start()

    def last(s):
        far = origin(RIGHT, 4)
        for i in range(NCH // 2):
            for way in (RIGHT, LEFT):
                ring(s, 4, way, HALF_OF[way][i], far).wait_recv()
        share(s, 7, far, core).start()

    half = TOKENS // 2

    def across_chunk(chunk):
        across(chunk, 1 - yh).wait_recv()
        start_chunk(1, chunk)

    def near_start():
        for d in range(1, NYL):
            x_near(d, yl).start()

    def near_pass(e):
        x_near(e, (yl + NYL - e) % NYL).wait_recv()
        for d in range(1, NX):
            x_far(d, e, x).start()

    def x_wait():
        for d in range(1, NX):
            for e in range(NYL):
                x_far(d, e, (x + NX - d) % NX).wait_recv()

    def transpose(s_):
        at = pl.multiple_of(side(s_) * half, half)
        for i in range(half // 256):
            xt[:, pl.ds(i * 256, 256)] = xs[pl.ds(at + i * 256, 256), :].T

    def outer(s_, first, n):
        at = pl.ds(pl.multiple_of(side(s_) * half, half), half)

        @pl.loop(first, first + n)
        def _(i):
            cols = pl.ds(pl.multiple_of(i * PIECE, PIECE), PIECE)
            value = jnp.dot(xt[...], h[at, cols], preferred_element_type=F32)
            if s_ == 0:
                wg[:, cols] = value
            else:
                wg[:, cols] += value

    far = origin(RIGHT, 4)
    for step in PLAN:
        what, n = step[0], [int(i) for i in step[1:]]
        if what == "f":
            forward(*n)
        elif what == "l":
            last(*n)
        elif what == "a":
            across_chunk(*n)
        elif what == "c":
            share(1, 0, z, core).start()
        elif what == "p":
            if n[1] == 0:
                product(n[0], 0, z)
            elif n[1] == 4:
                product(n[0], 7, far)
            else:
                products(*n)
        elif what == "r":
            if n[1] == 0:
                reduce_x(n[0], z)
            elif n[1] == 4:
                reduce_x(n[0], far)
            else:
                reduce_pair(*n)
        elif what == "n":
            near_start()
        elif what == "x":
            near_pass(*n)
        elif what == "w":
            x_wait()
        elif what == "t":
            transpose(*n)
        elif what == "o":
            outer(*n)

    total = g_fin[...]
    for d in range(1, NYL):
        copy(s_out.at[0], s_in.at[d - 1], gy_send.at[0], gy_recv.at[d - 1], sibling).wait_recv()
        total = total + s_in[d - 1].astype(F32)
    ig_ref[...] = total.astype(BF16)

    for chunk in range(NCH):
        across(chunk, yh).wait_send()
    for s in (0, 1):
        for way in (RIGHT, LEFT):
            for k in range(1, 5):
                for chunk in range(NCH):
                    if k < 4 or chunk in HALF_OF[way]:
                        ring(s, k, way, chunk, z).wait_send()
        for slot in range(8):
            share(s, slot, z, core).wait_send()
    for d in range(1, NYL):
        x_near(d, yl).wait_send()
    for d in range(1, NX):
        for e in range(NYL):
            x_far(d, e, x).wait_send()

    @pl.loop(0, NYH * NZ)
    def _(at):
        @pl.when(at // NYL != x)
        def _():
            copy(g_out.at[at], g_in.at[0, 0], gx_send.at[at], gx_recv.at[0, 0], sibling).wait_send()

    @pl.loop(0, NYL)
    def _(j):
        @pl.when(j != yl)
        def _():
            copy(s_out.at[j], s_in.at[0], gy_send.at[j], gy_recv.at[0], sibling).wait_send()


def shards(inputs, preact, out_grad, weight):
    vmem = pl.BlockSpec(memory_space=pltpu.VMEM)
    hbm = pl.BlockSpec(memory_space=pltpu.HBM)
    dma = pltpu.SemaphoreType.DMA
    operands = [pltpu.with_memory_space_constraint(a, pltpu.HBM) for a in (inputs, preact, out_grad, weight)]
    return pl.pallas_call(
        kernel,
        out_shape=(pltpu.VMEM((TOK, WID), BF16), pltpu.VMEM((WID, HID), F32)),
        in_specs=[hbm, hbm, hbm, hbm],
        out_specs=(vmem, vmem),
        scratch_shapes=[
            pltpu.VMEM((ROWS, HID), BF16),
            pltpu.VMEM((ROWS, HID), BF16),
            pltpu.VMEM((TOKENS, HID), BF16),
            pltpu.VMEM((TOKENS, WID), BF16),
            pltpu.VMEM((WID, HID), BF16),
            pltpu.VMEM((WID, TOKENS // 2), BF16),
            pltpu.VMEM((NYL, TOK, WID), F32),
            pltpu.VMEM((NYH * NZ, TOK, WID), BF16),
            pltpu.VMEM((NX - 1, NYL, TOK, WID), BF16),
            pltpu.VMEM((NYL, TOK, WID), BF16),
            pltpu.VMEM((NYL - 1, TOK, WID), BF16),
            pltpu.VMEM((TOK, WID), F32),
            dma((4,)),
            dma((NCH,)), dma((NCH,)),
            dma((2, 2, 5, NCH)), dma((2, 2, 5, NCH)),
            dma((2, 8)), dma((2, 8)),
            dma((NYL - 1,)), dma((NYL - 1,)),
            dma((NX - 1, NYL)), dma((NX - 1, NYL)),
            dma((NYH * NZ,)), dma((NX - 1, NYL)),
            dma((NYL,)), dma((NYL - 1,)),
        ],
        compiler_params=pltpu.CompilerParams(
            collective_id=0, has_side_effects=True, vmem_limit_bytes=48 << 20
        ),
        cost_estimate=pl.CostEstimate(
            flops=4 * TOKENS * HID * WID, bytes_accessed=8 << 20, transcendentals=ROWS * HID
        ),
    )(*operands)


def solution(mesh):
    in_specs = (P("col", "row"), P("row", "col"), P("row", "col"), P("row", "col"))
    out_specs = (P("col", "row"), P("row", "col"))
    return jax.shard_map(shards, mesh=mesh, in_specs=in_specs, out_specs=out_specs, check_vma=False)
```

time: 97.2 us -> 77.6 us (0.80)
  Pallas kernels: 90.1 us -> 74.7 us
  local copies, waits for them, and re-layouts: 6.06 us -> 2.05 us
    pallas_call x1, Pallas kernels: 90.1 us -> 74.7 us  [shards(): pl.pallas_call(kernel, out_shape=(pltpu.VMEM((TOK, WID), BF16), pltpu.VME...]
    unnamed x10 -> x2, local copies, waits for them, and re-layouts: 6.06 us -> 2.05 us
where the time goes in v2:
time: 77.6 us; the launch traced here: 77.4 us
  Pallas kernels  74.7 us (96%)
  local copies, waits for them, and re-layouts  2.05 us (3%)
    pallas_call x1, Pallas kernels, shards(): pl.pallas_call(kernel, out_shape=(pltpu.VMEM((TOK, WID), BF16), pltpu.VME...  74.7 us
    unnamed x2, local copies, waits for them, and re-layouts  2.05 us

profile of v2, /device:TPU:6, one launch (start us, length us, event | category | flops | bytes accessed | tf_op | source)
XLA Modules:
  0.0 77.4 jit_solution(1754195266047378835)
XLA Ops:
  0.6 74.7 %shard_map.59 = (bf16[128,384]{1,0:T(8,128)(2,1)S(1)}, f32[384,1536]{1,0:T(8,128)S(1)}) custom-call(bf16[128,384]{1,0:T(8,128)(2,1)} %x_hbm.1, bf16[64,1536]{1,0:T(8,128)(2,1)} %pre_hbm.1, bf16[64,1536]{1,0:T(8,128)(2,1)} %grad_hbm.1, bf16[384,1536]{1,0:T(8,128)(2,1)} %w_hbm.1), custom_call_target="tpu_custom_call" | custom-call | flops 4831838208 | bytes 8388608 | tf_op jit(solution)/shard_map/pallas_call | solution.py:324
  75.4 0.6 copy.8
  76.0 1.4 %copy.9 = f32[384,1536]{1,0:T(8,128)} copy(f32[384,1536]{1,0:T(8,128)S(1)} %get-tuple-element.3) | data formatting | bytes 4718592

commit v3 on v2

--- a/solution.py
+++ b/solution.py
@@ -13,13 +13,14 @@
 
 NX, NYL, NYH, NZ = 4, 4, 2, 8
 ROWS, HID, WID = 64, 1536, 384
-NCH = 4
+NCH = 2
 CHUNK = ROWS // NCH
 PIECE = 384
 TOK = 2 * ROWS
 TOKENS = TOK * NYH * NZ
 RIGHT, LEFT = 0, 1
-PLAN = ('p00', 'f01', 'f02', 'a0', 'a1', 'a2', 'a3', 'c', 'n', 'p01', 'f03', 'p02', 'p10', 'l0', 'f11', 'x1', 'x2', 'x3', 'p03', 'p04', 'f12', 'p11', 'r00', 'r01', 'r02', 'f13', 'p12', 'p13', 'r03', 'r04', 'r10', 'l1', 'p14', 'w', 'r11', 'r12', 't0', 'o004', 'r13', 'r14', 't1', 'o104')
+PLAN = ('p00', 'f01', 'f02', 'a0', 'a1', 'c', 'n', 'p01', 'f11', 'p02', 'p10', 'f12', 'x1', 'x2', 'x3', 'p11', 'f03', 'p12', 'p03', 'f13', 'p13', 'l0', 'p04', 'l1', 'p14', 'w', 't0', 'o004', 'r00', 'q00', 'r01', 'q01', 'r02', 'q02', 'r10', 'q10', 'r11', 'q11', 'r12', 'q12', 'r03', 'q03', 'r13', 'q13', 'r04', 'q04', 'r14', 'q14', 'd', 't1', 'o104')
+SPLIT = ((0, 3), (0, 4), (1, 1), (1, 2), (1, 3), (1, 4))
 HALF_OF = {RIGHT: range(NCH // 2), LEFT: range(NCH // 2, NCH)}
 
 
@@ -34,15 +35,16 @@
 
 def kernel(
     x_hbm, pre_hbm, grad_hbm, w_hbm, ig_ref, wg,
-    pre, grad, h, xs, w, xt, g_own, g_out, g_in, s_out, s_in, g_fin,
+    pre, grad, h, xs, w, xt, g_own, g_out, g_in, s_out, s_in, g_fin, b_own, b_in, b_out, b_far, b_fin,
     in_sem,
     hy_send, hy_recv, hz_send, hz_recv, hc_send, hc_recv,
     xy_send, xy_recv, xx_send, xx_recv,
-    gx_send, gx_recv, gy_send, gy_recv,
+    gx_send, gx_recv, gy_send, gy_recv, by_send, by_recv, bx_send, bx_recv,
 ):
     r, c = lax.axis_index("row"), lax.axis_index("col")
     yh, z, core = r // (2 * NZ), (r // 2) % NZ, r % 2
     x, yl = c // NYL, c % NYL
+    split = frozenset(SPLIT)
 
     def dev(yh_=yh, z_=z, core_=core, x_=x, yl_=yl):
         return ((yh_ * NZ + z_) * 2 + core_, x_ * NYL + yl_)
@@ -135,18 +137,31 @@
     def home(s, z_from):
         return side(s) * (NZ // NYL) + z_from // NYL, z_from % NYL
 
-    def part_out(s, z_from, x_to, j):
+    def top(s, k):
+        return pl.ds(0, ROWS if (s, k) in split else TOK)
+
+    low = pl.ds(ROWS, ROWS)
+
+    def part_out(s, k, z_from, x_to, j):
         d = (x + NX - x_to) % NX
         at = side(s) * NZ + z_from
         return copy(
-            g_out.at[at], g_in.at[d - 1, j], gx_send.at[at], gx_recv.at[d - 1, j], dev(x_=x_to)
+            g_out.at[at, top(s, k)], g_in.at[d - 1, j, top(s, k)], gx_send.at[at], gx_recv.at[d - 1, j],
+            dev(x_=x_to),
         )
 
-    def product(s, slot, z_from):
+    def low_out(s, z_from, x_to, j):
+        d = (yl + NYL - j) % NYL
+        at = side(s) * NZ + z_from
+        return copy(g_out.at[at, low], b_in.at[d - 1, x_to], by_send.at[at], by_recv.at[d - 1, x_to], dev(yl_=j))
+
+    def product(s, k, slot, z_from):
         share(s, slot, z_from, 1 - core).wait_recv()
-        at = pl.ds(pl.multiple_of((side(s) * NZ + z_from) * TOK, TOK), TOK)
-        part = lax.dot_general(h[at, :], w[...], (((1,), (1,)), ((), ())), preferred_element_type=F32)
+        at = side(s) * NZ + z_from
+        rows_at = pl.ds(pl.multiple_of(at * TOK, TOK), TOK)
+        part = lax.dot_general(h[rows_at, :], w[...], (((1,), (1,)), ((), ())), preferred_element_type=F32)
         x_to, j = home(s, z_from)
+        g_out[at] = part.astype(BF16)
 
         @pl.when(x_to == x)
         def _():
@@ -154,42 +169,88 @@
 
         @pl.when(x_to != x)
         def _():
-            g_out[side(s) * NZ + z_from] = part.astype(BF16)
-            part_out(s, z_from, x_to, j).start()
-
-    def both(fn):
-        @pl.loop(0, 2)
-        def _(i):
-            fn(i)
+            part_out(s, k, z_from, x_to, j).start()
+
+        if (s, k) in split:
+            @pl.when(j == yl)
+            def _():
+                b_own[x_to] = part[ROWS:, :]
+
+            @pl.when(j != yl)
+            def _():
+                low_out(s, z_from, x_to, j).start()
+
+    def each(k, fn):
+        if k == 0:
+            fn(0, z)
+        elif k == 4:
+            fn(7, origin(RIGHT, 4))
+        else:
+            @pl.loop(0, 2)
+            def _(i):
+                fn(k + 3 * i, (z + NZ + (2 * i - 1) * k) % NZ)
 
     def products(s, k):
-        both(lambda i: product(s, k + 3 * i, (z + NZ + (2 * i - 1) * k) % NZ))
-
-    def sum_out(j):
+        each(k, lambda slot, z_from: product(s, k, slot, z_from))
+
+    def sum_out(s, k, j):
         d = (yl + NYL - j) % NYL
-        return copy(s_out.at[j], s_in.at[d - 1], gy_send.at[j], gy_recv.at[d - 1], dev(yl_=j))
-
-    def reduce_x(s, z_from):
-        x_to, j = home(s, z_from)
-
-        @pl.when(x_to == x)
-        def _():
-            total = g_own[j]
-            for d in range(1, NX):
-                copy(g_out.at[0], g_in.at[d - 1, j], gx_send.at[0], gx_recv.at[d - 1, j], sibling).wait_recv()
-                total = total + g_in[d - 1, j].astype(F32)
+        return copy(
+            s_out.at[j, top(s, k)], s_in.at[d - 1, top(s, k)], gy_send.at[j], gy_recv.at[d - 1], dev(yl_=j)
+        )
+
+    def low_sum(x_to):
+        d = (x + NX - x_to) % NX
+        return copy(b_out.at[x_to], b_far.at[d - 1], bx_send.at[x_to], bx_recv.at[d - 1], dev(x_=x_to))
+
+    def reduce_x(s, k):
+        rows_ = top(s, k)
+
+        def one(slot, z_from):
+            x_to, j = home(s, z_from)
+
+            @pl.when(x_to == x)
+            def _():
+                total = g_own[j, rows_]
+                for d in range(1, NX):
+                    here = g_in.at[d - 1, j, rows_]
+                    copy(here, here, gx_send.at[0], gx_recv.at[d - 1, j], sibling).wait_recv()
+                    total = total + here[...].astype(F32)
+
+                @pl.when(j == yl)
+                def _():
+                    g_fin[rows_] = total
+
+                @pl.when(j != yl)
+                def _():
+                    s_out[j, rows_] = total.astype(BF16)
+                    sum_out(s, k, j).start()
+
+        each(k, one)
+
+    def reduce_y(s, k):
+        def one(slot, z_from):
+            x_to, j = home(s, z_from)
 
             @pl.when(j == yl)
             def _():
-                g_fin[...] = total
-
-            @pl.when(j != yl)
-            def _():
-                s_out[j] = total.astype(BF16)
-                sum_out(j).start()
-
-    def reduce_pair(s, k):
-        both(lambda i: reduce_x(s, (z + NZ + (2 * i - 1) * k) % NZ))
+                total = b_own[x_to]
+                for d in range(1, NYL):
+                    here = b_in.at[d - 1, x_to]
+                    copy(here, here, by_send.at[0], by_recv.at[d - 1, x_to], sibling).wait_recv()
+                    total = total + here[...].astype(F32)
+
+                @pl.when(x_to == x)
+                def _():
+                    b_fin[...] = total
+
+                @pl.when(x_to != x)
+                def _():
+                    b_out[x_to] = total.astype(BF16)
+                    low_sum(x_to).start()
+
+        if (s, k) in split:
+            each(k, one)
 
     def forward(s, k):
         for chunk in range(NCH):
@@ -245,7 +306,46 @@
             else:
                 wg[:, cols] += value
 
-    far = origin(RIGHT, 4)
+    def drain():
+        for chunk in range(NCH):
+            across(chunk, yh).wait_send()
+        for s in (0, 1):
+            for way in (RIGHT, LEFT):
+                for k in range(1, 5):
+                    for chunk in range(NCH):
+                        if k < 4 or chunk in HALF_OF[way]:
+                            ring(s, k, way, chunk, z).wait_send()
+            for slot in range(8):
+                share(s, slot, z, core).wait_send()
+        for d in range(1, NYL):
+            x_near(d, yl).wait_send()
+        for d in range(1, NX):
+            for e in range(NYL):
+                x_far(d, e, x).wait_send()
+
+    def sent(s, k):
+        def one(slot, z_from):
+            x_to, j = home(s, z_from)
+
+            @pl.when(x_to != x)
+            def _():
+                part_out(s, k, z_from, x_to, j).wait_send()
+
+            @pl.when((x_to == x) & (j != yl))
+            def _():
+                sum_out(s, k, j).wait_send()
+
+            if (s, k) in split:
+                @pl.when(j != yl)
+                def _():
+                    low_out(s, z_from, x_to, j).wait_send()
+
+                @pl.when((j == yl) & (x_to != x))
+                def _():
+                    low_sum(x_to).wait_send()
+
+        each(k, one)
+
     for step in PLAN:
         what, n = step[0], [int(i) for i in step[1:]]
         if what == "f":
@@ -257,19 +357,11 @@
         elif what == "c":
             share(1, 0, z, core).start()
         elif what == "p":
-            if n[1] == 0:
-                product(n[0], 0, z)
-            elif n[1] == 4:
-                product(n[0], 7, far)
-            else:
-                products(*n)
+            products(*n)
         elif what == "r":
-            if n[1] == 0:
-                reduce_x(n[0], z)
-            elif n[1] == 4:
-                reduce_x(n[0], far)
-            else:
-                reduce_pair(*n)
+            reduce_x(*n)
+        elif what == "q":
+            reduce_y(*n)
         elif what == "n":
             near_start()
         elif what == "x":
@@ -280,40 +372,37 @@
             transpose(*n)
         elif what == "o":
             outer(*n)
-
-    total = g_fin[...]
-    for d in range(1, NYL):
-        copy(s_out.at[0], s_in.at[d - 1], gy_send.at[0], gy_recv.at[d - 1], sibling).wait_recv()
-        total = total + s_in[d - 1].astype(F32)
-    ig_ref[...] = total.astype(BF16)
-
-    for chunk in range(NCH):
-        across(chunk, yh).wait_send()
+        elif what == "d":
+            drain()
+
+    def finish(rows_, first, arrived, recv):
+        total = first
+        for d in range(1, NYL):
+            here = arrived.at[d - 1, rows_]
+            copy(here, here, gy_send.at[0], recv.at[d - 1], sibling).wait_recv()
+            total = total + here[...].astype(F32)
+        return total.astype(BF16)
+
+    def final(s, k):
+        def one(slot, z_from):
+            x_to, j = home(s, z_from)
+
+            @pl.when((x_to == x) & (j == yl))
+            def _():
+                rows_ = top(s, k)
+                ig_ref[rows_, :] = finish(rows_, g_fin[rows_], s_in, gy_recv)
+                if (s, k) in split:
+                    all_ = pl.ds(0, ROWS)
+                    ig_ref[low, :] = finish(all_, b_fin[...], b_far, bx_recv)
+
+        each(k, one)
+
     for s in (0, 1):
-        for way in (RIGHT, LEFT):
-            for k in range(1, 5):
-                for chunk in range(NCH):
-                    if k < 4 or chunk in HALF_OF[way]:
-                        ring(s, k, way, chunk, z).wait_send()
-        for slot in range(8):
-            share(s, slot, z, core).wait_send()
-    for d in range(1, NYL):
-        x_near(d, yl).wait_send()
-    for d in range(1, NX):
-        for e in range(NYL):
-            x_far(d, e, x).wait_send()
-
-    @pl.loop(0, NYH * NZ)
-    def _(at):
-        @pl.when(at // NYL != x)
-        def _():
-            copy(g_out.at[at], g_in.at[0, 0], gx_send.at[at], gx_recv.at[0, 0], sibling).wait_send()
-
-    @pl.loop(0, NYL)
-    def _(j):
-        @pl.when(j != yl)
-        def _():
-            copy(s_out.at[j], s_in.at[0], gy_send.at[j], gy_recv.at[0], sibling).wait_send()
+        for k in range(5):
+            sent(s, k)
+    for s in (0, 1):
+        for k in range(5):
+            final(s, k)
 
 
 def shards(inputs, preact, out_grad, weight):
@@ -339,6 +428,11 @@
             pltpu.VMEM((NYL, TOK, WID), BF16),
             pltpu.VMEM((NYL - 1, TOK, WID), BF16),
             pltpu.VMEM((TOK, WID), F32),
+            pltpu.VMEM((NX, ROWS, WID), F32),
+            pltpu.VMEM((NYL - 1, NX, ROWS, WID), BF16),
+            pltpu.VMEM((NX, ROWS, WID), BF16),
+            pltpu.VMEM((NX - 1, ROWS, WID), BF16),
+            pltpu.VMEM((ROWS, WID), F32),
             dma((4,)),
             dma((NCH,)), dma((NCH,)),
             dma((2, 2, 5, NCH)), dma((2, 2, 5, NCH)),
@@ -347,6 +441,8 @@
             dma((NX - 1, NYL)), dma((NX - 1, NYL)),
             dma((NYH * NZ,)), dma((NX - 1, NYL)),
             dma((NYL,)), dma((NYL - 1,)),
+            dma((NYH * NZ,)), dma((NYL - 1, NX)),
+            dma((NX,)), dma((NX - 1,)),
         ],
         compiler_params=pltpu.CompilerParams(
             collective_id=0, has_side_effects=True, vmem_limit_bytes=48 << 20

time: 77.6 us -> 69.8 us (0.90)
  the two profiles are of different devices: /device:TPU:6 before, /device:TPU:4 now
where the time goes in v3:
time: 69.8 us; the launch traced here: 69.6 us
  Pallas kernels  66.9 us (96%)
  local copies, waits for them, and re-layouts  2.05 us (3%)
    pallas_call x1, Pallas kernels, shards(): pl.pallas_call(kernel, out_shape=(pltpu.VMEM((TOK, WID), BF16), pltpu.VME...  66.9 us
    unnamed x2, local copies, waits for them, and re-layouts  2.05 us

profile of v3, /device:TPU:4, one launch (start us, length us, event | category | flops | bytes accessed | tf_op | source)
XLA Modules:
  0.0 69.6 jit_solution(8814519270599775065)
XLA Ops:
  0.6 66.9 %shard_map.59 = (bf16[128,384]{1,0:T(8,128)(2,1)S(1)}, f32[384,1536]{1,0:T(8,128)S(1)}) custom-call(bf16[128,384]{1,0:T(8,128)(2,1)} %x_hbm.1, bf16[64,1536]{1,0:T(8,128)(2,1)} %pre_hbm.1, bf16[64,1536]{1,0:T(8,128)(2,1)} %grad_hbm.1, bf16[384,1536]{1,0:T(8,128)(2,1)} %w_hbm.1), custom_call_target="tpu_custom_call" | custom-call | flops 4831838208 | bytes 8388608 | tf_op jit(solution)/shard_map/pallas_call | solution.py:413
  67.6 0.6 copy.8
  68.2 1.4 %copy.9 = f32[384,1536]{1,0:T(8,128)} copy(f32[384,1536]{1,0:T(8,128)S(1)} %get-tuple-element.3) | data formatting | bytes 4718592

commit v4 on v3

--- a/solution.py
+++ b/solution.py
@@ -19,8 +19,13 @@
 TOK = 2 * ROWS
 TOKENS = TOK * NYH * NZ
 RIGHT, LEFT = 0, 1
-PLAN = ('p00', 'f01', 'f02', 'a0', 'a1', 'c', 'n', 'p01', 'f11', 'p02', 'p10', 'f12', 'x1', 'x2', 'x3', 'p11', 'f03', 'p12', 'p03', 'f13', 'p13', 'l0', 'p04', 'l1', 'p14', 'w', 't0', 'o004', 'r00', 'q00', 'r01', 'q01', 'r02', 'q02', 'r10', 'q10', 'r11', 'q11', 'r12', 'q12', 'r03', 'q03', 'r13', 'q13', 'r04', 'q04', 'r14', 'q14', 'd', 't1', 'o104')
-SPLIT = ((0, 3), (0, 4), (1, 1), (1, 2), (1, 3), (1, 4))
+PLAN = (
+    "p00", "f01", "f02", "a0", "a1", "c", "n", "p01", "f11", "p02", "p10", "x1", "x2", "x3", "f12", "p11",
+    "f03", "p12", "p03", "f13", "p13", "l0", "p04", "l1", "p14", "w", "t0", "o004", "r00", "q00", "r01",
+    "q01", "r02", "q02", "r10", "q10", "r11", "q11", "r12", "q12", "r03", "q03", "r13", "q13", "r04", "q04",
+    "r14", "q14", "d", "t1", "o104",
+)
+SPLIT = tuple((s, k) for s in (0, 1) for k in range(5))
 HALF_OF = {RIGHT: range(NCH // 2), LEFT: range(NCH // 2, NCH)}
 
 
@@ -35,7 +40,7 @@
 
 def kernel(
     x_hbm, pre_hbm, grad_hbm, w_hbm, ig_ref, wg,
-    pre, grad, h, xs, w, xt, g_own, g_out, g_in, s_out, s_in, g_fin, b_own, b_in, b_out, b_far, b_fin,
+    pre, grad, h, xs, w, wt, xt, g_own, g_out, g_in, s_out, s_in, g_fin, b_own, b_in, b_out, b_far, b_fin,
     in_sem,
     hy_send, hy_recv, hz_send, hz_recv, hc_send, hc_recv,
     xy_send, xy_recv, xx_send, xx_recv,
@@ -133,6 +138,9 @@
     for d in range(1, NX):
         x_far(d, 0, x).start()
     w_copy.wait()
+    for i in range(HID // 256):
+        at = pl.ds(i * 256, 256)
+        wt[at, :] = w[:, at].T
 
     def home(s, z_from):
         return side(s) * (NZ // NYL) + z_from // NYL, z_from % NYL
@@ -159,7 +167,7 @@
         share(s, slot, z_from, 1 - core).wait_recv()
         at = side(s) * NZ + z_from
         rows_at = pl.ds(pl.multiple_of(at * TOK, TOK), TOK)
-        part = lax.dot_general(h[rows_at, :], w[...], (((1,), (1,)), ((), ())), preferred_element_type=F32)
+        part = jnp.dot(h[rows_at, :], wt[...], preferred_element_type=F32)
         x_to, j = home(s, z_from)
         g_out[at] = part.astype(BF16)
 
@@ -421,6 +429,7 @@
             pltpu.VMEM((TOKENS, HID), BF16),
             pltpu.VMEM((TOKENS, WID), BF16),
             pltpu.VMEM((WID, HID), BF16),
+            pltpu.VMEM((HID, WID), BF16),
             pltpu.VMEM((WID, TOKENS // 2), BF16),
             pltpu.VMEM((NYL, TOK, WID), F32),
             pltpu.VMEM((NYH * NZ, TOK, WID), BF16),

time: 69.8 us -> 66.3 us (0.950)
  the two profiles are of different devices: /device:TPU:4 before, /device:TPU:6 now
where the time goes in v4:
time: 66.3 us; the launch traced here: 65.3 us
  Pallas kernels  62.7 us (95%)
  local copies, waits for them, and re-layouts  2.05 us (3%)
    pallas_call x1, Pallas kernels, shards(): pl.pallas_call(kernel, out_shape=(pltpu.VMEM((TOK, WID), BF16), pltpu.VME...  62.7 us
    unnamed x2, local copies, waits for them, and re-layouts  2.05 us

profile of v4, /device:TPU:6, one launch (start us, length us, event | category | flops | bytes accessed | tf_op | source)
XLA Modules:
  0.0 65.3 jit_solution(5048279469032884480)
XLA Ops:
  0.6 62.7 %shard_map.59 = (bf16[128,384]{1,0:T(8,128)(2,1)S(1)}, f32[384,1536]{1,0:T(8,128)S(1)}) custom-call(bf16[128,384]{1,0:T(8,128)(2,1)} %x_hbm.1, bf16[64,1536]{1,0:T(8,128)(2,1)} %pre_hbm.1, bf16[64,1536]{1,0:T(8,128)(2,1)} %grad_hbm.1, bf16[384,1536]{1,0:T(8,128)(2,1)} %w_hbm.1), custom_call_target="tpu_custom_call" | custom-call | flops 4831838208 | bytes 8388608 | tf_op jit(solution)/shard_map/pallas_call | solution.py:421
  63.3 0.6 copy.8
  63.9 1.4 %copy.9 = f32[384,1536]{1,0:T(8,128)} copy(f32[384,1536]{1,0:T(8,128)S(1)} %get-tuple-element.3) | data formatting | bytes 4718592
